TPU v7x, 32 devices: a whole 2x2x4 slice. The times are simulated.
32 devices in a mesh: freq: 2 (over x), space: 16 (over z, y, core).
Axes of the slice: x: 2, y: 2, z: 4, core: 2. Of those that a mesh axis runs over, the one named last changes fastest.
Arguments:
- rhs: float32 [2, 5, 256, 1024], P(None, None, ('freq', 'space')), parts along dimension 2, may hold values from -12 to 12
- inv_diag: float32 [2, 5, 5, 256, 1024], P(None, None, None, ('freq', 'space')), parts along dimension 3
- face_coef: float32 [4, 256, 1024], P(None, ('freq', 'space')), parts along dimension 1, may hold values from 0.6 to 1.8
- flux_jac: float32 [2, 5, 5], replicated, may hold values from -1.8 to 1.8
- press_weights: float32 [5], replicated, may hold values from -4 to 4
- surface_cells: int32 [8192], P('space'), may hold values from 0 to 8191, as said below
- interface_slot: int32 [8192], P('space'), may hold values from 0 to 8191, as said below
- mode_shapes: float32 [8192, 192], P('space'), may hold values from -0.09375 to 0.09375
Outputs:
- state: float32 [2, 5, 256, 1024], P(None, None, ('freq', 'space')), parts along dimension 2
- forces: float32 [2, 384], P(None, ('freq', 'space')), parts along dimension 1
There are 2 independent parts, one for each index of `freq`. A program takes and returns all parts, laid end to end along the dimension named above; an argument that names none is the same for every part. Nothing has to cross between parts.
Inputs may be any that keep to these rules, and one draw needn't show every extreme that they name: `surface_cells`: the 512 entries held by one device are distinct cell indices of that device; on some device they include both its first and its last cell. `interface_slot`: A permutation of all 8192 interface indices; the owner of index i is device i // 512 of space, and each device holds exactly the same number of rows of every owner.
All inputs are finite; a program needn't handle non-finite values.
Results may differ from a plain program's by a relative error of at most 0.0003.
Values sent between devices are 32-bit elements; how exact they have to be, the bound alone decides.
A program may use at most 64 MiB of HBM per device.

v0:
```python
import jax
import jax.numpy as jnp
from jax import lax
from jax.sharding import PartitionSpec as P

ITERS = 8


def with_halo(block, sides, width):
    for axis, dim in sides:
        count = lax.axis_size(axis)
        forward = [(i, i + 1) for i in range(count - 1)]
        backward = [(target, source) for source, target in forward]
        low = lax.ppermute(
            lax.slice_in_dim(block, block.shape[dim] - width, None, axis=dim), axis, forward
        )
        high = lax.ppermute(lax.slice_in_dim(block, 0, width, axis=dim), axis, backward)
        block = jnp.concatenate([low, block, high], axis=dim)
    return block


def block_apply(inv_diag, vector):
    real_part = jnp.sum(inv_diag[0] * vector[0][None], axis=1) - jnp.sum(
        inv_diag[1] * vector[1][None], axis=1
    )
    imag_part = jnp.sum(inv_diag[0] * vector[1][None], axis=1) + jnp.sum(
        inv_diag[1] * vector[0][None], axis=1
    )
    return jnp.stack([real_part, imag_part])


def couple(extended, face_coef, flux_jac):
    middle = extended[:, :, 1:-1, :]
    along_planes = face_coef[0] * extended[:, :, 2:, :] + face_coef[1] * extended[:, :, :-2, :]
    padded = jnp.pad(middle, ((0, 0), (0, 0), (0, 0), (1, 1)))
    along_cells = face_coef[2] * padded[..., 2:] + face_coef[3] * padded[..., :-2]
    mixed = jnp.einsum("kj,rjpq->rkpq", flux_jac[0], along_planes, precision=lax.Precision.HIGHEST)
    return mixed + jnp.einsum(
        "kj,rjpq->rkpq", flux_jac[1], along_cells, precision=lax.Precision.HIGHEST
    )


def sweep(extended, inv_diag, rhs, face_coef, flux_jac):
    return block_apply(inv_diag, rhs + couple(extended, face_coef, flux_jac))


def local(
    rhs, inv_diag, face_coef, flux_jac, press_weights, surface_cells, interface_slot, mode_shapes
):
    planes = rhs.shape[2]
    width_cells = rhs.shape[3]
    state = block_apply(inv_diag, rhs)
    for sweep_index in range(ITERS):
        extended = with_halo(state, (("space", 2),), 1)
        state = sweep(extended, inv_diag, rhs, face_coef, flux_jac)
    cells = state.reshape(2, 5, planes * width_cells)
    pressure = jnp.sum(press_weights[None, :, None] * cells, axis=1)
    surface = jnp.take(pressure, surface_cells, axis=1)
    row_count = interface_slot.shape[0]
    ranking = jnp.argsort(interface_slot)
    outgoing = jnp.take(surface, ranking, axis=1)
    local_index = (jnp.take(interface_slot, ranking) % row_count)[None]
    arrived, arrived_index = (
        lax.all_to_all(outgoing, "space", split_axis=1, concat_axis=1, tiled=True),
        lax.all_to_all(local_index, "space", split_axis=1, concat_axis=1, tiled=True),
    )
    placed = jnp.zeros((2, row_count), jnp.float32).at[:, arrived_index[0]].set(arrived)
    partial_forces = jnp.dot(
        placed, mode_shapes, precision=lax.Precision.HIGHEST, preferred_element_type=jnp.float32
    )
    total_forces = lax.psum(partial_forces, "space")
    share = partial_forces.shape[1] // lax.axis_size("space")
    forces = lax.dynamic_slice_in_dim(total_forces, lax.axis_index("space") * share, share, 1)
    return (state, forces)


def solution(mesh):
    in_specs = (
        P(None, None, ("freq", "space"), None),
        P(None, None, None, ("freq", "space"), None),
        P(None, ("freq", "space"), None),
        P(),
        P(),
        P("space"),
        P("space"),
        P("space", None),
    )
    out_specs = (P(None, None, ("freq", "space"), None), P(None, ("freq", "space")))
    return jax.shard_map(local, mesh=mesh, in_specs=in_specs, out_specs=out_specs, check_vma=False)
```

profile of v0, /device:TPU:0, one launch (start us, length us, event | category | flops | bytes accessed | tf_op | source)
XLA Modules:
  0.0 153.9 jit_solution(311613572397250854)
XLA Ops:
  0.6 1.1 slice_bitcast_fusion.16
  1.8 1.7 %fusion.17 = (f32[5,8,1024]{2,1,0:T(8,128)S(1)}, f32[5,8,1024]{2,1,0:T(8,128)S(1)}, f32[5,8,1024]{2,1,0:T(8,128)S(1)}, f32[5,8,1024]{2,1,0:T(8,128)S(1)}) fusion(f32[5,8,1024]{2,1,0:T(8,128)S(1)} %get-tuple-element.109, f32[2,5,5,8,1024]{4,3,2,1,0:T(8,128)} %param.9, f32[5,8,1024]{2,1,0:T(8,128)S(1)} %get-tuple-element.108), kind=kLoop, calls=%fused_computation.47 | loop fusion | flops 1474560 | bytes 2621440 | tf_op jit(solution)/shard_map/reduce_sum | solution.py:26
  3.6 1.4 collective-permute-start
  5.0 3.0 %collective-permute-start.1 = (f32[2,5,1,1024]{3,2,1,0:T(1,128)S(1)}, f32[2,5,1,1024]{3,2,1,0:T(1,128)S(1)}, u32[]{:S(2)}, u32[]{:S(2)}) collective-permute-start(f32[2,5,1,1024]{3,2,1,0:T(1,128)S(1)} %get-tuple-element.107), channel_id=1, source_target_pairs={{0,1},{1,2},{2,3},{3,4},{4,5},{5,6},{6,7},{7,8},{8,9},{9,10},{10,1... | collective-permute-start | bytes 122888 | tf_op jit(solution)/shard_map/ppermute | solution.py:14
  8.2 3.8 %sort.17 = (s32[512]{0:T(512)}, s32[512]{0:T(512)S(1)}) sort(s32[512]{0:T(512)S(1)} %copy-done.1, s32[512]{0:T(512)S(1)} %iota.4), dimensions={0}, to_apply=%region_36.37 | sort | flops 4608 | bytes 8192 | tf_op jit(solution)/shard_map/jit(argsort)/sort | solution.py:60
  12.1 0.7 fusion.75
  13.1 0.9 fusion.15
  14.5 0.3 fusion.19
  14.9 1.3 collective-permute-start.2
  16.2 5.1 %collective-permute-start.3 = (f32[2,5,1,1024]{3,2,1,0:T(1,128)S(1)}, f32[2,5,1,1024]{3,2,1,0:T(1,128)S(1)}, u32[]{:S(2)}, u32[]{:S(2)}) collective-permute-start(f32[2,5,1,1024]{3,2,1,0:T(1,128)S(1)} %get-tuple-element.103), channel_id=1, source_target_pairs={{0,1},{1,2},{2,3},{3,4},{4,5},{5,6},{6,7},{7,8},{8,9},{9,10},{10,1... | collective-permute-start | bytes 122888 | tf_op jit(solution)/shard_map/ppermute | solution.py:14
  21.4 3.5 %gather_fusion = s32[512]{0:T(512)S(1)} fusion(s32[512]{0:T(512)S(1)} %copy-done.1, s32[1024]{0:T(1024)S(1)} %pad_clamp_fusion.1), kind=kCustom, calls=%fused_computation | custom fusion | bytes 6144 | tf_op jit(solution)/shard_map/jit(_take)/gather | solution.py:62
  25.3 0.7 fusion.72
  26.0 0.9 fusion.13
  27.2 0.3 fusion.21
  27.6 1.3 collective-permute-start.4
  28.9 4.3 %collective-permute-start.5 = (f32[2,5,1,1024]{3,2,1,0:T(1,128)S(1)}, f32[2,5,1,1024]{3,2,1,0:T(1,128)S(1)}, u32[]{:S(2)}, u32[]{:S(2)}) collective-permute-start(f32[2,5,1,1024]{3,2,1,0:T(1,128)S(1)} %get-tuple-element.99), channel_id=1, source_target_pairs={{0,1},{1,2},{2,3},{3,4},{4,5},{5,6},{6,7},{7,8},{8,9},{9,10},{10,1... | collective-permute-start | bytes 122888 | tf_op jit(solution)/shard_map/ppermute | solution.py:14
  33.3 0.7 collective-permute-done.5
  34.4 0.7 fusion.69
  35.2 0.9 fusion.11
  36.4 0.3 fusion.23
  36.8 1.3 collective-permute-start.6
  38.1 4.5 %collective-permute-start.7 = (f32[2,5,1,1024]{3,2,1,0:T(1,128)S(1)}, f32[2,5,1,1024]{3,2,1,0:T(1,128)S(1)}, u32[]{:S(2)}, u32[]{:S(2)}) collective-permute-start(f32[2,5,1,1024]{3,2,1,0:T(1,128)S(1)} %get-tuple-element.95), channel_id=1, source_target_pairs={{0,1},{1,2},{2,3},{3,4},{4,5},{5,6},{6,7},{7,8},{8,9},{9,10},{10,1... | collective-permute-start | bytes 122888 | tf_op jit(solution)/shard_map/ppermute | solution.py:14
  42.6 0.6 and_select_fusion
  43.2 10.4 %all-to-all-start = ((s32[1,16,32]{2,0,1:T(1,128)}), s32[1,16,32]{2,0,1:T(1,128)S(1)}, u32[]{:S(2)}, u32[]{:S(2)}) async-start(s32[1,16,32]{2,0,1:T(1,128)} %and_select_fusion), calls=%async_computation | async-start | bytes 16384 | tf_op jit(solution)/shard_map/all_to_all | solution.py:65
  54.0 0.7 fusion.66
  54.8 0.9 fusion.9
  56.0 0.3 fusion.25
  56.4 1.3 collective-permute-start.8
  57.7 3.0 %collective-permute-start.9 = (f32[2,5,1,1024]{3,2,1,0:T(1,128)S(1)}, f32[2,5,1,1024]{3,2,1,0:T(1,128)S(1)}, u32[]{:S(2)}, u32[]{:S(2)}) collective-permute-start(f32[2,5,1,1024]{3,2,1,0:T(1,128)S(1)} %get-tuple-element.91), channel_id=1, source_target_pairs={{0,1},{1,2},{2,3},{3,4},{4,5},{5,6},{6,7},{7,8},{8,9},{9,10},{10,1... | collective-permute-start | bytes 122888 | tf_op jit(solution)/shard_map/ppermute | solution.py:14
  60.7 0.8 collective-permute-done.9
  62.0 0.7 fusion.63
  62.7 0.9 fusion.7
  63.9 0.3 fusion.27
  64.3 1.3 collective-permute-start.10
  65.6 4.4 %collective-permute-start.11 = (f32[2,5,1,1024]{3,2,1,0:T(1,128)S(1)}, f32[2,5,1,1024]{3,2,1,0:T(1,128)S(1)}, u32[]{:S(2)}, u32[]{:S(2)}) collective-permute-start(f32[2,5,1,1024]{3,2,1,0:T(1,128)S(1)} %get-tuple-element.87), channel_id=1, source_target_pairs={{0,1},{1,2},{2,3},{3,4},{4,5},{5,6},{6,7},{7,8},{8,9},{9,10},{10,1... | collective-permute-start | bytes 122888 | tf_op jit(solution)/shard_map/ppermute | solution.py:14
  70.0 0.8 collective-permute-done.11
  71.2 0.7 fusion.60
  72.0 0.9 fusion.5
  73.2 0.3 fusion.29
  73.6 1.3 collective-permute-start.12
  74.9 5.4 %collective-permute-start.13 = (f32[2,5,1,1024]{3,2,1,0:T(1,128)S(1)}, f32[2,5,1,1024]{3,2,1,0:T(1,128)S(1)}, u32[]{:S(2)}, u32[]{:S(2)}) collective-permute-start(f32[2,5,1,1024]{3,2,1,0:T(1,128)S(1)} %get-tuple-element.83), channel_id=1, source_target_pairs={{0,1},{1,2},{2,3},{3,4},{4,5},{5,6},{6,7},{7,8},{8,9},{9,10},{10,1... | collective-permute-start | bytes 122888 | tf_op jit(solution)/shard_map/ppermute | solution.py:14
  80.4 0.5 broadcast.113
  80.9 0.7 reduce.3
  82.0 0.7 fusion.57
  82.8 0.9 fusion.3
  84.0 0.3 fusion.31
  84.4 1.3 collective-permute-start.14
  85.7 5.2 %collective-permute-start.15 = (f32[2,5,1,1024]{3,2,1,0:T(1,128)S(1)}, f32[2,5,1,1024]{3,2,1,0:T(1,128)S(1)}, u32[]{:S(2)}, u32[]{:S(2)}) collective-permute-start(f32[2,5,1,1024]{3,2,1,0:T(1,128)S(1)} %get-tuple-element.79), channel_id=1, source_target_pairs={{0,1},{1,2},{2,3},{3,4},{4,5},{5,6},{6,7},{7,8},{8,9},{9,10},{10,1... | collective-permute-start | bytes 122888 | tf_op jit(solution)/shard_map/ppermute | solution.py:14
  90.9 0.6 collective-permute-done.15
  91.9 0.7 fusion.54
  92.7 0.9 fusion.1
  93.9 0.3 fusion.32
  94.5 0.2 fusion.52
  94.8 2.6 %copy.148 = f32[2,8192]{0,1:T(8,128)} copy(f32[2,8192]{1,0:T(2,128)S(1)} %fusion.52) | data formatting | bytes 131072 | tf_op jit(solution)/shard_map/reduce_sum | solution.py:57
  97.4 3.2 %gather_fusion.1 = f32[512,2]{1,0:T(8,128)S(1)} fusion(f32[2,8192]{0,1:T(8,128)} %copy.148, s32[1024]{0:T(1024)S(1)} %pad_clamp_fusion), kind=kCustom, calls=%fused_computation.1 | custom fusion | bytes 10240 | tf_op jit(solution)/shard_map/jit(_take)/gather | solution.py:58
  100.8 1.0 gather_fusion.2
  102.0 0.6 broadcast_select_fusion
  102.6 11.9 %all-to-all-start.1 = ((f32[2,16,32]{2,0,1:T(2,128)}), f32[2,16,32]{2,0,1:T(2,128)S(1)}, u32[]{:S(2)}, u32[]{:S(2)}) async-start(f32[2,16,32]{2,0,1:T(2,128)} %broadcast_select_fusion), calls=%async_computation.1 | async-start | bytes 32768 | tf_op jit(solution)/shard_map/all_to_all | solution.py:64
  114.5 0.7 pad_maximum_fusion.40
  115.3 5.7 %all-to-all-done.1 = f32[2,16,32]{2,0,1:T(2,128)S(1)} async-done(((f32[2,16,32]{2,0,1:T(2,128)}), f32[2,16,32]{2,0,1:T(2,128)S(1)}, u32[]{:S(2)}, u32[]{:S(2)}) %all-to-all-start.1) | async-done | bytes 4128 | tf_op jit(solution)/shard_map/all_to_all | solution.py:64
  121.2 1.8 %scatter_custom_fusion = f32[2,512]{0,1:T(8,128)S(1)} fusion(s32[512]{0:T(512)S(1)} %bitcast.262, f32[512,2]{1,0:T(8,128)S(1)} %copy.151, f32[]{:T(128)} %constant.46.clone.1), kind=kCustom, calls=%fused_computation.298 | custom fusion | bytes 4100 | tf_op jit(solution)/shard_map/scatter | solution.py:67
  123.0 0.5 fusion.145
  123.6 29.7 %psum.7 = f32[2,192]{1,0:T(2,128)S(1)} all-reduce(f32[2,192]{1,0:T(2,128)S(1)} %fusion.145), channel_id=1, replica_groups=mesh['freq'=2,'space'=16] {'space'}, use_global_device_ids=true, to_apply=%region_39.40 | all-reduce | flops 384 | bytes 3072 | tf_op jit(solution)/shard_map/psum | solution.py:71
  153.3 0.6 constant_dynamic-slice_fusion
  (114 shorter events, 7.3 us)
Async XLA Ops:
  0.6 122.4 %copy-start = (f32[512,192]{0,1:T(8,128)S(1)}, f32[512,192]{0,1:T(8,128)}, u32[]{:S(2)}) copy-start(f32[512,192]{0,1:T(8,128)} %param.15) | copy-start | bytes 1179652
  1.7 6.4 %copy-start.4 = (f32[4,8,1024]{2,1,0:T(8,128)S(1)}, f32[4,8,1024]{2,1,0:T(8,128)}, u32[]{:S(2)}) copy-start(f32[4,8,1024]{2,1,0:T(8,128)} %param.10) | copy-start | bytes 393220
  1.7 6.4 %copy-start.6 = (f32[2,5,5]{2,0,1:T(2,128)S(1)}, f32[2,5,5]{2,0,1:T(2,128)}, u32[]{:S(2)}) copy-start(f32[2,5,5]{2,0,1:T(2,128)} %param.11) | copy-start | bytes 604
  1.7 6.4 %copy-start.1 = (s32[512]{0:T(512)S(1)}, s32[512]{0:T(512)}, u32[]{:S(2)}) copy-start(s32[512]{0:T(512)} %param.14) | copy-start | bytes 6148
  3.6 9.5 %copy-start.3 = (f32[2,5,8,1024]{3,2,1,0:T(8,128)S(1)}, f32[2,5,8,1024]{3,2,1,0:T(8,128)}, u32[]{:S(2)}) copy-start(f32[2,5,8,1024]{3,2,1,0:T(8,128)} %param.8) | copy-start | bytes 983044
  3.6 8.3 %collective-permute-start = (f32[2,5,1,1024]{3,2,1,0:T(1,128)S(1)}, f32[2,5,1,1024]{3,2,1,0:T(1,128)S(1)}, u32[]{:S(2)}, u32[]{:S(2)}) collective-permute-start(f32[2,5,1,1024]{3,2,1,0:T(1,128)S(1)} %get-tuple-element.106), channel_id=1, source_target_pairs={{1,0},{2,1},{3,2},{4,3},{5,4},{6,5},{7,6},{8,7},{9,8},{10,9},{11,1... | collective-permute-start | bytes 122888 | tf_op jit(solution)/shard_map/ppermute | solution.py:17
  5.0 6.9 %collective-permute-start.1 = (f32[2,5,1,1024]{3,2,1,0:T(1,128)S(1)}, f32[2,5,1,1024]{3,2,1,0:T(1,128)S(1)}, u32[]{:S(2)}, u32[]{:S(2)}) collective-permute-start(f32[2,5,1,1024]{3,2,1,0:T(1,128)S(1)} %get-tuple-element.107), channel_id=1, source_target_pairs={{0,1},{1,2},{2,3},{3,4},{4,5},{5,6},{6,7},{7,8},{8,9},{9,10},{10,1... | collective-permute-start | bytes 122888 | tf_op jit(solution)/shard_map/ppermute | solution.py:14
  13.1 1.4 copy-start.2
  14.9 9.9 %collective-permute-start.2 = (f32[2,5,1,1024]{3,2,1,0:T(1,128)S(1)}, f32[2,5,1,1024]{3,2,1,0:T(1,128)S(1)}, u32[]{:S(2)}, u32[]{:S(2)}) collective-permute-start(f32[2,5,1,1024]{3,2,1,0:T(1,128)S(1)} %get-tuple-element.102), channel_id=1, source_target_pairs={{1,0},{2,1},{3,2},{4,3},{5,4},{6,5},{7,6},{8,7},{9,8},{10,9},{11,1... | collective-permute-start | bytes 122888 | tf_op jit(solution)/shard_map/ppermute | solution.py:17
  16.2 8.7 %collective-permute-start.3 = (f32[2,5,1,1024]{3,2,1,0:T(1,128)S(1)}, f32[2,5,1,1024]{3,2,1,0:T(1,128)S(1)}, u32[]{:S(2)}, u32[]{:S(2)}) collective-permute-start(f32[2,5,1,1024]{3,2,1,0:T(1,128)S(1)} %get-tuple-element.103), channel_id=1, source_target_pairs={{0,1},{1,2},{2,3},{3,4},{4,5},{5,6},{6,7},{7,8},{8,9},{9,10},{10,1... | collective-permute-start | bytes 122888 | tf_op jit(solution)/shard_map/ppermute | solution.py:14
  27.6 5.7 %collective-permute-start.4 = (f32[2,5,1,1024]{3,2,1,0:T(1,128)S(1)}, f32[2,5,1,1024]{3,2,1,0:T(1,128)S(1)}, u32[]{:S(2)}, u32[]{:S(2)}) collective-permute-start(f32[2,5,1,1024]{3,2,1,0:T(1,128)S(1)} %get-tuple-element.98), channel_id=1, source_target_pairs={{1,0},{2,1},{3,2},{4,3},{5,4},{6,5},{7,6},{8,7},{9,8},{10,9},{11,1... | collective-permute-start | bytes 122888 | tf_op jit(solution)/shard_map/ppermute | solution.py:17
  28.9 5.1 %collective-permute-start.5 = (f32[2,5,1,1024]{3,2,1,0:T(1,128)S(1)}, f32[2,5,1,1024]{3,2,1,0:T(1,128)S(1)}, u32[]{:S(2)}, u32[]{:S(2)}) collective-permute-start(f32[2,5,1,1024]{3,2,1,0:T(1,128)S(1)} %get-tuple-element.99), channel_id=1, source_target_pairs={{0,1},{1,2},{2,3},{3,4},{4,5},{5,6},{6,7},{7,8},{8,9},{9,10},{10,1... | collective-permute-start | bytes 122888 | tf_op jit(solution)/shard_map/ppermute | solution.py:14
  36.8 16.8 %collective-permute-start.6 = (f32[2,5,1,1024]{3,2,1,0:T(1,128)S(1)}, f32[2,5,1,1024]{3,2,1,0:T(1,128)S(1)}, u32[]{:S(2)}, u32[]{:S(2)}) collective-permute-start(f32[2,5,1,1024]{3,2,1,0:T(1,128)S(1)} %get-tuple-element.94), channel_id=1, source_target_pairs={{1,0},{2,1},{3,2},{4,3},{5,4},{6,5},{7,6},{8,7},{9,8},{10,9},{11,1... | collective-permute-start | bytes 122888 | tf_op jit(solution)/shard_map/ppermute | solution.py:17
  38.1 15.5 %collective-permute-start.7 = (f32[2,5,1,1024]{3,2,1,0:T(1,128)S(1)}, f32[2,5,1,1024]{3,2,1,0:T(1,128)S(1)}, u32[]{:S(2)}, u32[]{:S(2)}) collective-permute-start(f32[2,5,1,1024]{3,2,1,0:T(1,128)S(1)} %get-tuple-element.95), channel_id=1, source_target_pairs={{0,1},{1,2},{2,3},{3,4},{4,5},{5,6},{6,7},{7,8},{8,9},{9,10},{10,1... | collective-permute-start | bytes 122888 | tf_op jit(solution)/shard_map/ppermute | solution.py:14
  43.2 37.2 %all-to-all-start = ((s32[1,16,32]{2,0,1:T(1,128)}), s32[1,16,32]{2,0,1:T(1,128)S(1)}, u32[]{:S(2)}, u32[]{:S(2)}) async-start(s32[1,16,32]{2,0,1:T(1,128)} %and_select_fusion), calls=%async_computation | async-start | bytes 16384 | tf_op jit(solution)/shard_map/all_to_all | solution.py:65
  56.0 4.7 %copy-start.5 = (s32[512]{0:T(512)S(1)}, s32[512]{0:T(512)}, u32[]{:S(2)}) copy-start(s32[512]{0:T(512)} %param.13) | copy-start | bytes 6148
  56.4 4.4 %collective-permute-start.8 = (f32[2,5,1,1024]{3,2,1,0:T(1,128)S(1)}, f32[2,5,1,1024]{3,2,1,0:T(1,128)S(1)}, u32[]{:S(2)}, u32[]{:S(2)}) collective-permute-start(f32[2,5,1,1024]{3,2,1,0:T(1,128)S(1)} %get-tuple-element.90), channel_id=1, source_target_pairs={{1,0},{2,1},{3,2},{4,3},{5,4},{6,5},{7,6},{8,7},{9,8},{10,9},{11,1... | collective-permute-start | bytes 122888 | tf_op jit(solution)/shard_map/ppermute | solution.py:17
  57.7 3.9 %collective-permute-start.9 = (f32[2,5,1,1024]{3,2,1,0:T(1,128)S(1)}, f32[2,5,1,1024]{3,2,1,0:T(1,128)S(1)}, u32[]{:S(2)}, u32[]{:S(2)}) collective-permute-start(f32[2,5,1,1024]{3,2,1,0:T(1,128)S(1)} %get-tuple-element.91), channel_id=1, source_target_pairs={{0,1},{1,2},{2,3},{3,4},{4,5},{5,6},{6,7},{7,8},{8,9},{9,10},{10,1... | collective-permute-start | bytes 122888 | tf_op jit(solution)/shard_map/ppermute | solution.py:14
  64.3 5.7 %collective-permute-start.10 = (f32[2,5,1,1024]{3,2,1,0:T(1,128)S(1)}, f32[2,5,1,1024]{3,2,1,0:T(1,128)S(1)}, u32[]{:S(2)}, u32[]{:S(2)}) collective-permute-start(f32[2,5,1,1024]{3,2,1,0:T(1,128)S(1)} %get-tuple-element.86), channel_id=1, source_target_pairs={{1,0},{2,1},{3,2},{4,3},{5,4},{6,5},{7,6},{8,7},{9,8},{10,9},{11,1... | collective-permute-start | bytes 122888 | tf_op jit(solution)/shard_map/ppermute | solution.py:17
  65.6 5.3 %collective-permute-start.11 = (f32[2,5,1,1024]{3,2,1,0:T(1,128)S(1)}, f32[2,5,1,1024]{3,2,1,0:T(1,128)S(1)}, u32[]{:S(2)}, u32[]{:S(2)}) collective-permute-start(f32[2,5,1,1024]{3,2,1,0:T(1,128)S(1)} %get-tuple-element.87), channel_id=1, source_target_pairs={{0,1},{1,2},{2,3},{3,4},{4,5},{5,6},{6,7},{7,8},{8,9},{9,10},{10,1... | collective-permute-start | bytes 122888 | tf_op jit(solution)/shard_map/ppermute | solution.py:14
  73.6 8.1 %collective-permute-start.12 = (f32[2,5,1,1024]{3,2,1,0:T(1,128)S(1)}, f32[2,5,1,1024]{3,2,1,0:T(1,128)S(1)}, u32[]{:S(2)}, u32[]{:S(2)}) collective-permute-start(f32[2,5,1,1024]{3,2,1,0:T(1,128)S(1)} %get-tuple-element.82), channel_id=1, source_target_pairs={{1,0},{2,1},{3,2},{4,3},{5,4},{6,5},{7,6},{8,7},{9,8},{10,9},{11,1... | collective-permute-start | bytes 122888 | tf_op jit(solution)/shard_map/ppermute | solution.py:17
  74.9 6.8 %collective-permute-start.13 = (f32[2,5,1,1024]{3,2,1,0:T(1,128)S(1)}, f32[2,5,1,1024]{3,2,1,0:T(1,128)S(1)}, u32[]{:S(2)}, u32[]{:S(2)}) collective-permute-start(f32[2,5,1,1024]{3,2,1,0:T(1,128)S(1)} %get-tuple-element.83), channel_id=1, source_target_pairs={{0,1},{1,2},{2,3},{3,4},{4,5},{5,6},{6,7},{7,8},{8,9},{9,10},{10,1... | collective-permute-start | bytes 122888 | tf_op jit(solution)/shard_map/ppermute | solution.py:14
  84.4 6.6 %collective-permute-start.14 = (f32[2,5,1,1024]{3,2,1,0:T(1,128)S(1)}, f32[2,5,1,1024]{3,2,1,0:T(1,128)S(1)}, u32[]{:S(2)}, u32[]{:S(2)}) collective-permute-start(f32[2,5,1,1024]{3,2,1,0:T(1,128)S(1)} %get-tuple-element.78), channel_id=1, source_target_pairs={{1,0},{2,1},{3,2},{4,3},{5,4},{6,5},{7,6},{8,7},{9,8},{10,9},{11,1... | collective-permute-start | bytes 122888 | tf_op jit(solution)/shard_map/ppermute | solution.py:17
  85.7 5.9 %collective-permute-start.15 = (f32[2,5,1,1024]{3,2,1,0:T(1,128)S(1)}, f32[2,5,1,1024]{3,2,1,0:T(1,128)S(1)}, u32[]{:S(2)}, u32[]{:S(2)}) collective-permute-start(f32[2,5,1,1024]{3,2,1,0:T(1,128)S(1)} %get-tuple-element.79), channel_id=1, source_target_pairs={{0,1},{1,2},{2,3},{3,4},{4,5},{5,6},{6,7},{7,8},{8,9},{9,10},{10,1... | collective-permute-start | bytes 122888 | tf_op jit(solution)/shard_map/ppermute | solution.py:14
  93.9 0.7 copy-start.7
  102.6 18.4 %all-to-all-start.1 = ((f32[2,16,32]{2,0,1:T(2,128)}), f32[2,16,32]{2,0,1:T(2,128)S(1)}, u32[]{:S(2)}, u32[]{:S(2)}) async-start(f32[2,16,32]{2,0,1:T(2,128)} %broadcast_select_fusion), calls=%async_computation.1 | async-start | bytes 32768 | tf_op jit(solution)/shard_map/all_to_all | solution.py:64
where the time goes:
time: 155 us; the launch traced here: 154 us
  starting transfers between devices  67.7 us (44%)
  blocking collectives  29.7 us (19%)
  local copies, waits for them, and re-layouts  17.5 us (11%)
  other arithmetic  14.6 us (9%)
  matrix products  13.9 us (9%)
  waiting for transfers between devices  8.78 us (6%)
  between operations  1.67 us (1%)
    ppermute x8, starting transfers between devices, with_halo(): lax.ppermute(lax.slice_in_dim(block, block.shape[dim] - width, None, axis...  35 us
    psum x1, blocking collectives, local(): total_forces = lax.psum(partial_forces, 'space')  29.7 us
    all_to_all x1, starting transfers between devices, local(): lax.all_to_all(outgoing, 'space', split_axis=1, concat_axis=1, tiled=True)  11.9 us
    ppermute x8, starting transfers between devices, with_halo(): lax.ppermute(lax.slice_in_dim(block, 0, width, axis=dim), axis, backward)  10.5 us
    all_to_all x1, starting transfers between devices, local(): lax.all_to_all(local_index, 'space', split_axis=1, concat_axis=1, tiled=T...  10.4 us
    dot_general x8, matrix products, couple(): jnp.einsum('kj,rjpq->rkpq', flux_jac[1], along_cells, precision=lax.Preci...  7.37 us
    dot_general x8, matrix products, couple(): jnp.einsum('kj,rjpq->rkpq', flux_jac[0], along_planes, precision=lax.Prec...  5.96 us
    all_to_all x1, waiting for transfers between devices, local(): lax.all_to_all(outgoing, 'space', split_axis=1, concat_axis=1, tiled=True)  5.75 us
  transfers between devices with their start and end apart: 18, of which 5 were waited for; matrix products, arithmetic and copies ran while one was open for 12% of the time, Pallas kernels for 0%

commit v1 on v0

v1 whole, which is shorter than its diff:
```python
import functools

import jax
import jax.numpy as jnp
from jax import lax
from jax.experimental import pallas as pl
from jax.experimental.pallas import tpu as pltpu
from jax.sharding import PartitionSpec as P

ITERS = 8
LANES = 128
COMP = 5
MESH = pl.DeviceIdType.MESH


def log2(value):
    assert value & (value - 1) == 0
    return value.bit_length() - 1


def thirds(x):
    a = x.astype(jnp.bfloat16)
    rest = x - a.astype(jnp.float32)
    b = rest.astype(jnp.bfloat16)
    c = (rest - b.astype(jnp.float32)).astype(jnp.bfloat16)
    return jnp.concatenate([a, b, c], axis=0)


def dot_exact(x, onehot, dims):
    rows = x.shape[0]
    out = lax.dot_general(thirds(x), onehot, (dims, ((), ())), preferred_element_type=jnp.float32)
    return (out[:rows] + out[rows : 2 * rows]) + out[2 * rows :]


def kernel(
    n, flux, press, rhs, inv, face, cells, slots, modes, state_out, forces_out,
    held, mixed, masked, send, halo, pressure, tiles, landed, part, parts,
    halo_send, halo_recv, tile_send, tile_recv, part_send, part_recv,
):
    planes, width = rhs.shape[2], rhs.shape[3]
    chunks = width // LANES
    rows = cells.shape[1]
    me = lax.axis_index("space")
    has_low, has_high = me > 0, me < n - 1

    barrier = pltpu.get_barrier_semaphore()

    def greet(d, carry):
        pl.semaphore_signal(
            barrier, inc=1, device_id={"space": lax.rem(me + d, n)}, device_id_type=MESH
        )
        return carry

    lax.fori_loop(1, n, greet, 0)

    row = lax.broadcasted_iota(jnp.int32, (planes, LANES), 0)
    lane = lax.broadcasted_iota(jnp.int32, (planes, LANES), 1)

    def at(c):
        return pl.ds(pl.multiple_of(c * LANES, LANES), LANES)

    def block_apply(c, z):
        out = []
        for k in range(COMP):
            real = imag = None
            for j in range(COMP):
                br, bi = inv[0, k, j, :, at(c)], inv[1, k, j, :, at(c)]
                re = br * z[j] - bi * z[COMP + j]
                im = br * z[COMP + j] + bi * z[j]
                real = re if real is None else real + re
                imag = im if imag is None else imag + im
            out.append((real, imag))
        return [o[0] for o in out] + [o[1] for o in out]

    def keep(c, sweep, values):
        for f in range(2 * COMP):
            held[c + 1, f] = values[f]
            send[sweep, 0, c, f] = values[f][planes - 1 :]
            send[sweep, 1, c, f] = values[f][:1]

    def first(c, carry):
        f0, f1 = face[0, :, at(c)], face[1, :, at(c)]
        zero = jnp.zeros_like(f0)
        masked[0, c] = jnp.where(row == planes - 1, zero, f0)
        masked[1, c] = jnp.where(row == 0, zero, f1)
        masked[2, c] = jnp.where(row == planes - 1, f0, zero)
        masked[3, c] = jnp.where(row == 0, f1, zero)
        z = [rhs[r, j, :, at(c)] for r in range(2) for j in range(COMP)]
        keep(c, 0, block_apply(c, z))
        return carry

    held[0] = jnp.zeros(held.shape[1:], jnp.float32)
    held[chunks + 1] = jnp.zeros(held.shape[1:], jnp.float32)

    @pl.when(jnp.logical_not(has_low))
    def _():
        for i in range(ITERS):
            halo[i, 0] = jnp.zeros(halo.shape[2:], jnp.float32)

    @pl.when(jnp.logical_not(has_high))
    def _():
        for i in range(ITERS):
            halo[i, 1] = jnp.zeros(halo.shape[2:], jnp.float32)

    lax.fori_loop(0, chunks, first, 0)
    pl.semaphore_wait(barrier, n - 1)

    def up(k):
        return pltpu.make_async_remote_copy(
            src_ref=send.at[k, 0], dst_ref=halo.at[k, 0],
            send_sem=halo_send.at[k, 0], recv_sem=halo_recv.at[k, 0],
            device_id={"space": me + 1}, device_id_type=MESH,
        )

    def down(k):
        return pltpu.make_async_remote_copy(
            src_ref=send.at[k, 1], dst_ref=halo.at[k, 1],
            send_sem=halo_send.at[k, 1], recv_sem=halo_recv.at[k, 1],
            device_id={"space": me - 1}, device_id_type=MESH,
        )

    def before(c, carry):
        f0, f1 = masked[0, c], masked[1, c]
        f2, f3 = face[2, :, at(c)], face[3, :, at(c)]
        for r in range(2):
            planewise, cellwise = [], []
            for j in range(COMP):
                f = r * COMP + j
                own = held[c + 1, f]
                after = pltpu.roll(jnp.where(lane == 0, held[c + 2, f], own), LANES - 1, 1)
                ahead = pltpu.roll(jnp.where(lane == LANES - 1, held[c, f], own), 1, 1)
                cellwise.append(f2 * after + f3 * ahead)
                planewise.append(f0 * pltpu.roll(own, planes - 1, 0) + f1 * pltpu.roll(own, 1, 0))
            for k in range(COMP):
                total = rhs[r, k, :, at(c)]
                for j in range(COMP):
                    total += flux[0, k, j] * planewise[j] + flux[1, k, j] * cellwise[j]
                mixed[c, r * COMP + k] = total
        return carry

    def sweep(s, carry):
        @pl.when(has_high)
        def _():
            up(s).start()

        @pl.when(has_low)
        def _():
            down(s).start()

        lax.fori_loop(0, chunks, before, 0)

        @pl.when(has_low)
        def _():
            up(s).wait_recv()
            down(s).wait_send()

        @pl.when(has_high)
        def _():
            down(s).wait_recv()
            up(s).wait_send()

        def behind(c, inner):
            e0, e1 = masked[2, c], masked[3, c]
            z = []
            for r in range(2):
                edge = [
                    e1 * halo[s, 0, c, r * COMP + j] + e0 * halo[s, 1, c, r * COMP + j]
                    for j in range(COMP)
                ]
                for k in range(COMP):
                    total = mixed[c, r * COMP + k]
                    for j in range(COMP):
                        total += flux[0, k, j] * edge[j]
                    z.append(total)
            keep(c, s + 1, block_apply(c, z))
            return inner

        lax.fori_loop(0, chunks, behind, 0)
        return carry

    lax.fori_loop(0, ITERS, sweep, 0)

    def finish(c, carry):
        for r in range(2):
            total = None
            for j in range(COMP):
                value = held[c + 1, r * COMP + j]
                state_out[r, j, :, at(c)] = value
                term = press[j] * value
                total = term if total is None else total + term
            pressure[r, c] = total
        return carry

    lax.fori_loop(0, chunks, finish, 0)

    cell = cells[...]
    grid = chunks * planes
    column = cell & (LANES - 1)
    place = ((cell & (width - 1)) >> log2(LANES)) * planes + (cell >> log2(width))
    pick = jnp.where(
        lax.broadcasted_iota(jnp.int32, (LANES, rows), 0) == column, 1.0, 0.0
    ).astype(jnp.bfloat16)
    flat = pressure[...].reshape(2 * grid, LANES)
    spread = dot_exact(flat, pick, ((1,), (0,)))
    here = lax.broadcasted_iota(jnp.int32, (grid, rows), 0) == place
    surface = [
        jnp.sum(jnp.where(here, spread[r * grid : (r + 1) * grid], 0.0), axis=0, keepdims=True)
        for r in range(2)
    ]

    slot = slots[...]
    deep = rows // LANES
    tall = 2 * deep
    index = lax.broadcasted_iota(jnp.int32, (n * tall, rows), 0)
    wanted = (index >> log2(tall)) * deep + (index & (deep - 1))
    value = jnp.where((index & (tall - 1)) < deep, surface[0], surface[1])
    value = jnp.where(wanted == (slot >> log2(LANES)), value, 0.0)
    put = jnp.where(
        lax.broadcasted_iota(jnp.int32, (LANES, rows), 0) == (slot & (LANES - 1)), 1.0, 0.0
    ).astype(jnp.bfloat16)
    tiles[...] = dot_exact(value, put, ((1,), (1,))).reshape(n, tall, LANES)

    def tile_copy(d):
        target = lax.rem(me + d, n)
        return pltpu.make_async_remote_copy(
            src_ref=tiles.at[target], dst_ref=landed.at[d],
            send_sem=tile_send.at[d], recv_sem=tile_recv.at[d],
            device_id={"space": target}, device_id_type=MESH,
        )

    def part_copy(d):
        return pltpu.make_async_remote_copy(
            src_ref=part, dst_ref=parts.at[d],
            send_sem=part_send.at[d], recv_sem=part_recv.at[d],
            device_id={"space": lax.rem(me + d, n)}, device_id_type=MESH,
        )

    def run(copy):
        def start(d, carry):
            copy(d).start()
            return carry

        def wait(d, carry):
            copy(d).wait()
            return carry

        lax.fori_loop(1, n, start, 0)
        lax.fori_loop(1, n, wait, 0)

    landed[0] = tiles[me]
    run(tile_copy)
    placed = jnp.sum(landed[...], axis=0)
    share = [None, None]
    for j in range(deep):
        product = jnp.dot(
            placed, modes[j * LANES : (j + 1) * LANES, :],
            precision=lax.Precision.HIGHEST, preferred_element_type=jnp.float32,
        )
        for r in range(2):
            term = product[r * deep + j : r * deep + j + 1]
            share[r] = term if share[r] is None else share[r] + term
    count = modes.shape[1]
    part[...] = jnp.zeros(part.shape, jnp.float32)
    for r in range(2):
        part[r : r + 1, :count] = share[r]
    parts[0] = part[...]
    run(part_copy)
    total = jnp.sum(parts[...], axis=0)[:, :count]
    mine = forces_out.shape[1]
    choose = (
        lax.broadcasted_iota(jnp.int32, (count, mine), 0)
        == lax.broadcasted_iota(jnp.int32, (count, mine), 1) + me * mine
    )
    forces_out[...] = dot_exact(
        total, jnp.where(choose, 1.0, 0.0).astype(jnp.bfloat16), ((1,), (0,))
    )[:2]


def local(
    rhs, inv_diag, face_coef, flux_jac, press_weights, surface_cells, interface_slot, mode_shapes
):
    n = lax.axis_size("space")
    planes, width = rhs.shape[2:]
    chunks = width // LANES
    rows, count = mode_shapes.shape
    tall = 2 * (rows // LANES)
    padded = -(-count // LANES) * LANES
    vmem = pl.BlockSpec(memory_space=pltpu.VMEM)
    smem = pl.BlockSpec(memory_space=pltpu.SMEM)
    f32 = jnp.float32
    dma = pltpu.SemaphoreType.DMA
    return pl.pallas_call(
        functools.partial(kernel, n),
        out_shape=(
            jax.ShapeDtypeStruct(rhs.shape, f32),
            jax.ShapeDtypeStruct((2, count // n), f32),
        ),
        in_specs=[smem, smem] + [vmem] * 6,
        out_specs=(vmem, vmem),
        scratch_shapes=[
            pltpu.VMEM((chunks + 2, 2 * COMP, planes, LANES), f32),
            pltpu.VMEM((chunks, 2 * COMP, planes, LANES), f32),
            pltpu.VMEM((4, chunks, planes, LANES), f32),
            pltpu.VMEM((ITERS + 1, 2, chunks, 2 * COMP, 1, LANES), f32),
            pltpu.VMEM((ITERS, 2, chunks, 2 * COMP, 1, LANES), f32),
            pltpu.VMEM((2, chunks, planes, LANES), f32),
            pltpu.VMEM((n, tall, LANES), f32),
            pltpu.VMEM((n, tall, LANES), f32),
            pltpu.VMEM((8, padded), f32),
            pltpu.VMEM((n, 8, padded), f32),
            dma((ITERS, 2)), dma((ITERS, 2)), dma((n,)), dma((n,)), dma((n,)), dma((n,)),
        ],
        compiler_params=pltpu.CompilerParams(
            collective_id=0, has_side_effects=True, vmem_limit_bytes=40 * 2**20
        ),
    )(
        flux_jac, press_weights, rhs, inv_diag, face_coef,
        surface_cells.reshape(1, rows), interface_slot.reshape(1, rows), mode_shapes,
    )


def solution(mesh):
    in_specs = (
        P(None, None, ("freq", "space"), None),
        P(None, None, None, ("freq", "space"), None),
        P(None, ("freq", "space"), None),
        P(),
        P(),
        P("space"),
        P("space"),
        P("space", None),
    )
    out_specs = (P(None, None, ("freq", "space"), None), P(None, ("freq", "space")))
    return jax.shard_map(local, mesh=mesh, in_specs=in_specs, out_specs=out_specs, check_vma=False)
```

time: 155 us -> 54 us (0.35)
  starting transfers between devices: 67.7 us -> 0 us
  Pallas kernels: 0 us -> 44.5 us
  blocking collectives: 29.7 us -> 0 us
  other arithmetic: 14.6 us -> 0 us
  matrix products: 13.9 us -> 0 us
  local copies, waits for them, and re-layouts: 17.5 us -> 8.49 us
  waiting for transfers between devices: 8.78 us -> 0 us
    ppermute x16 -> x0, starting transfers between devices: 45.4 us -> none  [the longest x8 35 us: with_halo(): lax.ppermute(lax.slice_in_dim(block, block.shape[dim] - width, None, axis...]
    pallas_call x0 -> x1, Pallas kernels: none -> 44.5 us  [local(): pl.pallas_call(functools.partial(kernel, n), out_shape=(jax.ShapeDtypeStr...]
    psum x1 -> x0, blocking collectives: 29.7 us -> none  [local(): total_forces = lax.psum(partial_forces, 'space')]
    all_to_all x2 -> x0, starting transfers between devices: 22.3 us -> none  [the longest x1 11.9 us: local(): lax.all_to_all(outgoing, 'space', split_axis=1, concat_axis=1, tiled=True)]
    dot_general x17 -> x0, matrix products: 13.9 us -> none  [the longest x8 7.37 us: couple(): jnp.einsum('kj,rjpq->rkpq', flux_jac[1], along_cells, precision=lax.Preci...]
    unnamed x16, local copies, waits for them, and re-layouts: 0.41 us -> 8.49 us
    gather x4 -> x0, local copies, waits for them, and re-layouts: 7.9 us -> none  [the longest x1 3.49 us: local(): local_index = (jnp.take(interface_slot, ranking) % row_count)[None]]
    all_to_all x2 -> x0, waiting for transfers between devices: 5.75 us -> none  [the longest x1 5.75 us: local(): lax.all_to_all(outgoing, 'space', split_axis=1, concat_axis=1, tiled=True)]
  transfers between devices with their start and end apart: 18 -> 0, of which waited for: 5 -> 0; matrix products, arithmetic and copies ran while one was open for 12% -> 0% of each run, Pallas kernels for 0% -> 0%
where the time goes in v1:
time: 54 us; the launch traced here: 53.7 us
  Pallas kernels  44.5 us (82%)
  local copies, waits for them, and re-layouts  8.49 us (16%)
  between operations  0.66 us (1%)
    pallas_call x1, Pallas kernels, local(): pl.pallas_call(functools.partial(kernel, n), out_shape=(jax.ShapeDtypeStr...  44.5 us
    unnamed x16, local copies, waits for them, and re-layouts  8.49 us

profile of v1, /device:TPU:0, one launch (start us, length us, event | category | flops | bytes accessed | tf_op | source)
XLA Modules:
  0.0 53.7 jit_solution(16366645750452353783)
XLA Ops:
  0.6 0.7 %copy.10.flux = f32[2,5,5]{2,1,0:T(8,128)S(1)} copy(f32[2,5,5]{2,0,1:T(2,128)} %param.11) | data formatting | bytes 400 | tf_op args[3]
  1.3 1.2 %copy.11.modes = f32[512,192]{1,0:T(8,128)S(1)} copy(f32[512,192]{0,1:T(8,128)} %param.15) | data formatting | bytes 786432 | tf_op args[7]
  2.5 0.0 copy-start
  2.5 1.4 %copy-done = f32[2,5,5,8,1024]{4,3,2,1,0:T(8,128)S(1)} copy-done((f32[2,5,5,8,1024]{4,3,2,1,0:T(8,128)S(1)}, f32[2,5,5,8,1024]{4,3,2,1,0:T(8,128)}, u32[]{:S(2)}) %copy-start) | copy-done | bytes 1638424
  4.0 0.0 copy-start.1
  4.0 1.0 %copy-done.1 = f32[2,5,8,1024]{3,2,1,0:T(8,128)S(1)} copy-done((f32[2,5,8,1024]{3,2,1,0:T(8,128)S(1)}, f32[2,5,8,1024]{3,2,1,0:T(8,128)}, u32[]{:S(2)}) %copy-start.1) | copy-done | bytes 327704
  4.9 0.0 copy-start.2
  4.9 0.9 %copy-done.2 = f32[4,8,1024]{2,1,0:T(8,128)S(1)} copy-done((f32[4,8,1024]{2,1,0:T(8,128)S(1)}, f32[4,8,1024]{2,1,0:T(8,128)}, u32[]{:S(2)}) %copy-start.2) | copy-done | bytes 131096
  5.8 0.0 copy-start.3
  5.8 0.7 %copy-done.3 = s32[512]{0:T(512)S(1)} copy-done((s32[512]{0:T(512)S(1)}, s32[512]{0:T(512)}, u32[]{:S(2)}) %copy-start.3) | copy-done | bytes 2072
  6.5 0.0 copy-start.4
  6.5 0.7 %copy-done.4 = s32[512]{0:T(512)S(1)} copy-done((s32[512]{0:T(512)S(1)}, s32[512]{0:T(512)}, u32[]{:S(2)}) %copy-start.4) | copy-done | bytes 2072
  7.2 0.0 copy-start.5
  7.2 0.7 %copy-done.5 = f32[5]{0:T(128)S(1)} copy-done((f32[5]{0:T(128)S(1)}, f32[5]{0:T(128)}, u32[]{:S(2)}) %copy-start.5) | copy-done | bytes 44
  7.9 44.5 %shard_map.95 = (f32[2,5,8,1024]{3,2,1,0:T(8,128)S(1)}, f32[2,12]{1,0:T(2,128)S(1)}) custom-call(f32[2,5,5]{2,1,0:T(8,128)S(1)} %copy.10.flux, f32[5]{0:T(128)S(1)} %copy-done.5, f32[2,5,8,1024]{3,2,1,0:T(8,128)S(1)} %copy-done.1, f32[2,5,5,8,1024]{4,3,2,1,0:T(8,128)S(1)} %copy-done, f32[4,8,1024]{2,1,0:T(8,128)S(1)} %copy-done.2, s32[1,512]{1,0:T(1,128)S(1)} %bitcast.2, ...), custom_call_target="tpu_custom_call" | custom-call | tf_op jit(solution)/shard_map/pallas_call | solution.py:292
  52.4 0.7 %copy.14 = f32[2,5,8,1024]{3,2,1,0:T(8,128)} copy(f32[2,5,8,1024]{3,2,1,0:T(8,128)S(1)} %get-tuple-element.4) | data formatting | bytes 655360
  53.1 0.6 %copy.15 = f32[2,12]{1,0:T(2,128)} copy(f32[2,12]{1,0:T(2,128)S(1)} %get-tuple-element.5) | data formatting | bytes 192
Async XLA Ops:
  2.5 1.4 %copy-start = (f32[2,5,5,8,1024]{4,3,2,1,0:T(8,128)S(1)}, f32[2,5,5,8,1024]{4,3,2,1,0:T(8,128)}, u32[]{:S(2)}) copy-start(f32[2,5,5,8,1024]{4,3,2,1,0:T(8,128)} %inv.1) | copy-start | bytes 4915204
  4.0 1.0 %copy-start.1 = (f32[2,5,8,1024]{3,2,1,0:T(8,128)S(1)}, f32[2,5,8,1024]{3,2,1,0:T(8,128)}, u32[]{:S(2)}) copy-start(f32[2,5,8,1024]{3,2,1,0:T(8,128)} %rhs.1) | copy-start | bytes 983044
  4.9 0.9 %copy-start.2 = (f32[4,8,1024]{2,1,0:T(8,128)S(1)}, f32[4,8,1024]{2,1,0:T(8,128)}, u32[]{:S(2)}) copy-start(f32[4,8,1024]{2,1,0:T(8,128)} %face.1) | copy-start | bytes 393220
  5.8 0.7 %copy-start.3 = (s32[512]{0:T(512)S(1)}, s32[512]{0:T(512)}, u32[]{:S(2)}) copy-start(s32[512]{0:T(512)} %param.13) | copy-start | bytes 6148
  6.5 0.7 %copy-start.4 = (s32[512]{0:T(512)S(1)}, s32[512]{0:T(512)}, u32[]{:S(2)}) copy-start(s32[512]{0:T(512)} %param.14) | copy-start | bytes 6148
  7.2 0.7 %copy-start.5 = (f32[5]{0:T(128)S(1)}, f32[5]{0:T(128)}, u32[]{:S(2)}) copy-start(f32[5]{0:T(128)} %press.1) | copy-start | bytes 64

commit v2 on v1

v2 whole, which is shorter than its diff:
```python
import functools

import jax
import jax.numpy as jnp
from jax import lax
from jax.experimental import pallas as pl
from jax.experimental.pallas import tpu as pltpu
from jax.sharding import PartitionSpec as P

ITERS = 8
LANES = 128
COMP = 5
MESH = pl.DeviceIdType.MESH


def log2(value):
    assert value & (value - 1) == 0
    return value.bit_length() - 1


def thirds(x):
    a = x.astype(jnp.bfloat16)
    rest = x - a.astype(jnp.float32)
    b = rest.astype(jnp.bfloat16)
    c = (rest - b.astype(jnp.float32)).astype(jnp.bfloat16)
    return jnp.concatenate([a, b, c], axis=0)


def dot_exact(x, onehot, dims):
    rows = x.shape[0]
    out = lax.dot_general(thirds(x), onehot, (dims, ((), ())), preferred_element_type=jnp.float32)
    return (out[:rows] + out[rows : 2 * rows]) + out[2 * rows :]


def kernel(
    n, flux, press, rhs_in, inv_in, face_in, cells_in, slots_in, modes_in, state_out, forces_out,
    rhs, inv, face, cells, slots, modes, loaded,
    held, mixed, masked, send, halo, fixed, beside, outer, pick, here, wanted, put,
    pressure, tiles, landed, part, parts,
    halo_send, halo_recv, fixed_send, fixed_recv,
    tile_send, tile_recv, part_send, part_recv,
):
    loads = [
        pltpu.make_async_copy(src, dst, loaded.at[i])
        for i, (src, dst) in enumerate(
            (
                (rhs_in, rhs), (inv_in, inv), (face_in, face),
                (cells_in, cells), (slots_in, slots), (modes_in, modes),
            )
        )
    ]
    for load in loads:
        load.start()
    planes, width = rhs.shape[2], rhs.shape[3]
    chunks = width // LANES
    rows = cells.shape[1]
    me = lax.axis_index("space")
    has_low, has_high = me > 0, me < n - 1

    barrier = pltpu.get_barrier_semaphore()

    def greet(d, carry):
        pl.semaphore_signal(
            barrier, inc=1, device_id={"space": lax.rem(me + d, n)}, device_id_type=MESH
        )
        return carry

    lax.fori_loop(1, n, greet, 0)

    row = lax.broadcasted_iota(jnp.int32, (planes, LANES), 0)
    lane = lax.broadcasted_iota(jnp.int32, (planes, LANES), 1)

    def at(c):
        return pl.ds(pl.multiple_of(c * LANES, LANES), LANES)

    def block_apply(block, z):
        reals, imags = [], []
        for k in range(COMP):
            real = imag = None
            for j in range(COMP):
                br, bi = block(k * COMP + j), block((COMP + k) * COMP + j)
                re = br * z[j] - bi * z[COMP + j]
                im = br * z[COMP + j] + bi * z[j]
                real = re if real is None else real + re
                imag = im if imag is None else imag + im
            reals.append(real)
            imags.append(imag)
        return reals + imags

    def own_block(c):
        return lambda i: inv[i // (COMP * COMP), i // COMP % COMP, i % COMP, :, at(c)]

    def keep(c, exchange, values):
        for f in range(2 * COMP):
            held[c + 1, f] = values[f]
            if exchange is not None:
                for p in range(2):
                    send[exchange, 0, p, f, pl.ds(c, 1)] = values[f][planes - 1 - p : planes - p]
                    send[exchange, 1, p, f, pl.ds(c, 1)] = values[f][p : p + 1]

    fields = 2 * COMP * COMP

    def first(c, carry):
        f0, f1 = face[0, :, at(c)], face[1, :, at(c)]
        zero = jnp.zeros_like(f0)
        masked[0, c] = jnp.where(row == planes - 1, zero, f0)
        masked[1, c] = jnp.where(row == 0, zero, f1)
        masked[2, c] = jnp.where(row == planes - 1, f0, zero)
        masked[3, c] = jnp.where(row == 0, f1, zero)
        z = [rhs[r, j, :, at(c)] for r in range(2) for j in range(COMP)]
        keep(c, 0, block_apply(own_block(c), z))
        block = own_block(c)
        f2, f3 = face[2, :, at(c)], face[3, :, at(c)]
        for i, x in enumerate([block(i) for i in range(fields)] + z):
            fixed[0, i, pl.ds(c, 1)] = x[planes - 1 :]
            fixed[1, i, pl.ds(c, 1)] = x[:1]
        for i, (x, y) in enumerate(((f0, f1), (f1, f0), (f2, f2), (f3, f3))):
            fixed[0, fields + 2 * COMP + i, pl.ds(c, 1)] = x[planes - 1 :]
            fixed[1, fields + 2 * COMP + i, pl.ds(c, 1)] = y[:1]
        return carry

    held[0] = jnp.zeros(held.shape[1:], jnp.float32)
    held[chunks + 1] = jnp.zeros(held.shape[1:], jnp.float32)

    @pl.when(jnp.logical_not(has_low))
    def _():
        beside[0] = jnp.zeros(beside.shape[1:], jnp.float32)
        for i in range(ITERS // 2):
            halo[i, 0] = jnp.zeros(halo.shape[2:], jnp.float32)

    @pl.when(jnp.logical_not(has_high))
    def _():
        beside[1] = jnp.zeros(beside.shape[1:], jnp.float32)
        for i in range(ITERS // 2):
            halo[i, 1] = jnp.zeros(halo.shape[2:], jnp.float32)

    for load in loads[:3]:
        load.wait()
    lax.fori_loop(0, chunks, first, 0)
    pl.semaphore_wait(barrier, n - 1)

    def state_copy(k, side):
        return pltpu.make_async_remote_copy(
            src_ref=send.at[k, side], dst_ref=halo.at[k, side],
            send_sem=halo_send.at[k, side], recv_sem=halo_recv.at[k, side],
            device_id={"space": me + 1 - 2 * side}, device_id_type=MESH,
        )

    def fixed_copy(side):
        return pltpu.make_async_remote_copy(
            src_ref=fixed.at[side], dst_ref=beside.at[side],
            send_sem=fixed_send.at[side], recv_sem=fixed_recv.at[side],
            device_id={"space": me + 1 - 2 * side}, device_id_type=MESH,
        )

    def exchange(k):
        for side, there in ((0, has_high), (1, has_low)):
            pl.when(there)(state_copy(k, side).start)

    exchange(0)
    for side, there in ((0, has_high), (1, has_low)):
        pl.when(there)(fixed_copy(side).start)

    def before(c, carry):
        f0, f1 = masked[0, c], masked[1, c]
        f2, f3 = face[2, :, at(c)], face[3, :, at(c)]
        for r in range(2):
            planewise, cellwise = [], []
            for j in range(COMP):
                f = r * COMP + j
                own = held[c + 1, f]
                after = pltpu.roll(jnp.where(lane == 0, held[c + 2, f], own), LANES - 1, 1)
                ahead = pltpu.roll(jnp.where(lane == LANES - 1, held[c, f], own), 1, 1)
                cellwise.append(f2 * after + f3 * ahead)
                planewise.append(f0 * pltpu.roll(own, planes - 1, 0) + f1 * pltpu.roll(own, 1, 0))
            for k in range(COMP):
                total = rhs[r, k, :, at(c)]
                for j in range(COMP):
                    total += flux[k, 0, j] * planewise[j] + flux[k, 1, j] * cellwise[j]
                mixed[c, r * COMP + k] = total
        return carry

    def behind(c, low, high, exchange):
        e0, e1 = masked[2, c], masked[3, c]
        z = []
        for r in range(2):
            edge = [e1 * low(r * COMP + j, c) + e0 * high(r * COMP + j, c) for j in range(COMP)]
            for k in range(COMP):
                total = mixed[c, r * COMP + k]
                for j in range(COMP):
                    total += flux[k, 0, j] * edge[j]
                z.append(total)
        keep(c, exchange, block_apply(own_block(c), z))

    chunk_row = lax.broadcasted_iota(jnp.int32, (chunks, LANES), 0)
    chunk_lane = lax.broadcasted_iota(jnp.int32, (chunks, LANES), 1)
    first_cell = (chunk_row == 0) & (chunk_lane == 0)
    last_cell = (chunk_row == chunks - 1) & (chunk_lane == LANES - 1)

    def sweep_outer(s, side):
        coefs = [beside[side, fields + 2 * COMP + i] for i in range(4)]
        z = []
        for r in range(2):
            planewise, cellwise = [], []
            for j in range(COMP):
                f = r * COMP + j
                x = halo[s, side, 0, f]
                after = pltpu.roll(
                    jnp.where(chunk_lane == 0, pltpu.roll(x, chunks - 1, 0), x), LANES - 1, 1
                )
                ahead = pltpu.roll(
                    jnp.where(chunk_lane == LANES - 1, pltpu.roll(x, 1, 0), x), 1, 1
                )
                cellwise.append(
                    coefs[2] * jnp.where(last_cell, 0.0, after)
                    + coefs[3] * jnp.where(first_cell, 0.0, ahead)
                )
                planewise.append(
                    coefs[0] * send[s, 1 - side, 0, f] + coefs[1] * halo[s, side, 1, f]
                )
            for k in range(COMP):
                total = beside[side, fields + r * COMP + k]
                for j in range(COMP):
                    total += flux[k, 0, j] * planewise[j] + flux[k, 1, j] * cellwise[j]
                z.append(total)
        values = block_apply(lambda i: beside[side, i], z)
        for f in range(2 * COMP):
            outer[side, f] = values[f]

    def two_sweeps(s, carry):
        lax.fori_loop(0, chunks, before, 0)
        for there, come, gone in ((has_low, 0, 1), (has_high, 1, 0)):
            @pl.when(there)
            def _():
                state_copy(s, come).wait_recv()
                state_copy(s, gone).wait_send()

            @pl.when(there & (s == 0))
            def _():
                fixed_copy(come).wait_recv()
                fixed_copy(gone).wait_send()

        def with_halo(c, inner):
            behind(
                c,
                lambda f, c: halo[s, 0, 0, f, pl.ds(c, 1)],
                lambda f, c: halo[s, 1, 0, f, pl.ds(c, 1)],
                None,
            )
            return inner

        lax.fori_loop(0, chunks, with_halo, 0)
        for side in range(2):
            sweep_outer(s, side)
        lax.fori_loop(0, chunks, before, 0)

        def with_outer(c, inner):
            behind(
                c,
                lambda f, c: outer[0, f, pl.ds(c, 1)],
                lambda f, c: outer[1, f, pl.ds(c, 1)],
                s + 1,
            )
            return inner

        lax.fori_loop(0, chunks, with_outer, 0)
        pl.when(s + 1 < ITERS // 2)(lambda: exchange(s + 1))
        return carry

    for load in loads[3:]:
        load.wait()
    cell, slot = cells[...], slots[...]
    grid = chunks * planes
    place = ((cell & (width - 1)) >> log2(LANES)) * planes + (cell >> log2(width))
    deep = rows // LANES
    tall = 2 * deep

    def count_rows(size):
        return lax.broadcasted_iota(jnp.int32, (size, rows), 0)

    def ones(where):
        return jnp.where(where, 1.0, 0.0)

    pick[...] = ones(count_rows(LANES) == (cell & (LANES - 1))).astype(jnp.bfloat16)
    put[...] = ones(count_rows(LANES) == (slot & (LANES - 1))).astype(jnp.bfloat16)
    here[...] = ones(count_rows(grid) == place)
    index = count_rows(n * tall)
    wanted[...] = ones(
        (index >> log2(tall)) * deep + (index & (deep - 1)) == (slot >> log2(LANES))
    )

    lax.fori_loop(0, ITERS // 2, two_sweeps, 0)

    def finish(c, carry):
        for r in range(2):
            total = None
            for j in range(COMP):
                value = held[c + 1, r * COMP + j]
                state_out[r, j, :, at(c)] = value
                term = press[j] * value
                total = term if total is None else total + term
            pressure[r, c] = total
        return carry

    lax.fori_loop(0, chunks, finish, 0)

    spread = dot_exact(pressure[...].reshape(2 * grid, LANES), pick[...], ((1,), (0,)))
    surface = [
        jnp.sum(here[...] * spread[r * grid : (r + 1) * grid], axis=0, keepdims=True)
        for r in range(2)
    ]
    value = wanted[...] * jnp.where(
        (count_rows(n * tall) & (tall - 1)) < deep, surface[0], surface[1]
    )
    tiles[...] = dot_exact(value, put[...], ((1,), (1,))).reshape(n, tall, LANES)

    def tile_copy(d):
        target = lax.rem(me + d, n)
        return pltpu.make_async_remote_copy(
            src_ref=tiles.at[target], dst_ref=landed.at[d],
            send_sem=tile_send.at[d], recv_sem=tile_recv.at[d],
            device_id={"space": target}, device_id_type=MESH,
        )

    def part_copy(d):
        return pltpu.make_async_remote_copy(
            src_ref=part, dst_ref=parts.at[d],
            send_sem=part_send.at[d], recv_sem=part_recv.at[d],
            device_id={"space": lax.rem(me + d, n)}, device_id_type=MESH,
        )

    def run(copy):
        def start(d, carry):
            copy(d).start()
            return carry

        def wait(d, carry):
            copy(d).wait()
            return carry

        lax.fori_loop(1, n, start, 0)
        lax.fori_loop(1, n, wait, 0)

    landed[0] = tiles[me]
    run(tile_copy)
    placed = jnp.sum(landed[...], axis=0)
    share = [None, None]
    for j in range(deep):
        product = lax.dot_general(
            placed, modes[:, j * LANES : (j + 1) * LANES], (((1,), (1,)), ((), ())),
            precision=lax.Precision.HIGHEST, preferred_element_type=jnp.float32,
        )
        for r in range(2):
            term = product[r * deep + j : r * deep + j + 1]
            share[r] = term if share[r] is None else share[r] + term
    count = modes.shape[0]
    part[...] = jnp.zeros(part.shape, jnp.float32)
    for r in range(2):
        part[r : r + 1, :count] = share[r]
    parts[0] = part[...]
    run(part_copy)
    total = jnp.sum(parts[...], axis=0)[:, :count]
    mine = forces_out.shape[1]
    choose = (
        lax.broadcasted_iota(jnp.int32, (count, mine), 0)
        == lax.broadcasted_iota(jnp.int32, (count, mine), 1) + me * mine
    )
    forces_out[...] = dot_exact(
        total, jnp.where(choose, 1.0, 0.0).astype(jnp.bfloat16), ((1,), (0,))
    )


def local(
    rhs, inv_diag, face_coef, flux_jac, press_weights, surface_cells, interface_slot, mode_shapes
):
    n = lax.axis_size("space")
    planes, width = rhs.shape[2:]
    chunks = width // LANES
    rows, count = mode_shapes.shape
    tall = 2 * (rows // LANES)
    padded = -(-count // LANES) * LANES
    vmem = pl.BlockSpec(memory_space=pltpu.VMEM)
    hbm = pl.BlockSpec(memory_space=pltpu.HBM)
    smem = pl.BlockSpec(memory_space=pltpu.SMEM)
    f32 = jnp.float32
    dma = pltpu.SemaphoreType.DMA
    return pl.pallas_call(
        functools.partial(kernel, n),
        out_shape=(
            jax.ShapeDtypeStruct(rhs.shape, f32),
            jax.ShapeDtypeStruct((2, count // n), f32),
        ),
        in_specs=[smem, smem] + [hbm] * 6,
        out_specs=(vmem, vmem),
        scratch_shapes=[
            pltpu.VMEM(rhs.shape, f32),
            pltpu.VMEM(inv_diag.shape, f32),
            pltpu.VMEM(face_coef.shape, f32),
            pltpu.VMEM((1, rows), jnp.int32),
            pltpu.VMEM((1, rows), jnp.int32),
            pltpu.VMEM((count, rows), f32),
            dma((6,)),
            pltpu.VMEM((chunks + 2, 2 * COMP, planes, LANES), f32),
            pltpu.VMEM((chunks, 2 * COMP, planes, LANES), f32),
            pltpu.VMEM((4, chunks, planes, LANES), f32),
            pltpu.VMEM((ITERS // 2 + 1, 2, 2, 2 * COMP, chunks, LANES), f32),
            pltpu.VMEM((ITERS // 2, 2, 2, 2 * COMP, chunks, LANES), f32),
            pltpu.VMEM((2, 2 * COMP * (COMP + 1) + 4, chunks, LANES), f32),
            pltpu.VMEM((2, 2 * COMP * (COMP + 1) + 4, chunks, LANES), f32),
            pltpu.VMEM((2, 2 * COMP, chunks, LANES), f32),
            pltpu.VMEM((LANES, rows), jnp.bfloat16),
            pltpu.VMEM((chunks * planes, rows), f32),
            pltpu.VMEM((n * tall, rows), f32),
            pltpu.VMEM((LANES, rows), jnp.bfloat16),
            pltpu.VMEM((2, chunks, planes, LANES), f32),
            pltpu.VMEM((n, tall, LANES), f32),
            pltpu.VMEM((n, tall, LANES), f32),
            pltpu.VMEM((2, padded), f32),
            pltpu.VMEM((n, 2, padded), f32),
            dma((ITERS // 2, 2)), dma((ITERS // 2, 2)), dma((2,)), dma((2,)), dma((n,)), dma((n,)), dma((n,)), dma((n,)),
        ],
        compiler_params=pltpu.CompilerParams(
            collective_id=0, has_side_effects=True, vmem_limit_bytes=63 * 2**20
        ),
    )(
        flux_jac.transpose(1, 0, 2), press_weights, rhs, inv_diag, face_coef,
        surface_cells.reshape(1, rows), interface_slot.reshape(1, rows), mode_shapes.T,
    )


def solution(mesh):
    in_specs = (
        P(None, None, ("freq", "space"), None),
        P(None, None, None, ("freq", "space"), None),
        P(None, ("freq", "space"), None),
        P(),
        P(),
        P("space"),
        P("space"),
        P("space", None),
    )
    out_specs = (P(None, None, ("freq", "space"), None), P(None, ("freq", "space")))
    return jax.shard_map(local, mesh=mesh, in_specs=in_specs, out_specs=out_specs, check_vma=False)
```

time: 54 us -> 48 us (0.89)
  local copies, waits for them, and re-layouts: 8.49 us -> 2.96 us
    unnamed x16 -> x2, local copies, waits for them, and re-layouts: 8.49 us -> 2.96 us
where the time goes in v2:
time: 48 us; the launch traced here: 47.8 us
  Pallas kernels  44.2 us (92%)
  local copies, waits for them, and re-layouts  2.96 us (6%)
  between operations  0.64 us (1%)
    pallas_call x1, Pallas kernels, local(): pl.pallas_call(functools.partial(kernel, n), out_shape=(jax.ShapeDtypeStr...  44.2 us
    unnamed x2, local copies, waits for them, and re-layouts  2.96 us

profile of v2, /device:TPU:0, one launch (start us, length us, event | category | flops | bytes accessed | tf_op | source)
XLA Modules:
  0.0 47.8 jit_solution(7980673611778312230)
XLA Ops:
  0.6 44.2 %shard_map.95 = (f32[2,5,8,1024]{3,2,1,0:T(8,128)}, f32[2,12]{1,0:T(2,128)}) custom-call(f32[5,2,5]{2,1,0:T(2,128)} %bitcast.5, f32[5]{0:T(128)} %press.1, f32[2,5,8,1024]{3,2,1,0:T(8,128)} %rhs_in.1, f32[2,5,5,8,1024]{4,3,2,1,0:T(8,128)} %inv_in.1, f32[4,8,1024]{2,1,0:T(8,128)} %face_in.1, s32[1,512]{1,0:T(1,128)} %bitcast.6, s32[1,512]{1,0:T(1,128)} %bitcast.7, ...), custom_call_target="tpu_custom_call" | custom-call | tf_op jit(solution)/shard_map/pallas_call | solution.py:387
  44.8 1.7 %copy.12 = f32[2,5,8,1024]{3,2,1,0:T(8,128)} copy(f32[2,5,8,1024]{3,2,1,0:T(8,128)} %get-tuple-element.4) | data formatting | bytes 655360
  46.5 1.2 %copy.13 = f32[2,12]{1,0:T(2,128)} copy(f32[2,12]{1,0:T(2,128)} %get-tuple-element.5) | data formatting | bytes 192

commit v3 on v2

--- a/solution.py
+++ b/solution.py
@@ -8,6 +8,7 @@
 from jax.sharding import PartitionSpec as P
 
 ITERS = 8
+UNROLL = 4
 LANES = 128
 COMP = 5
 MESH = pl.DeviceIdType.MESH
@@ -65,7 +66,7 @@
         )
         return carry
 
-    lax.fori_loop(1, n, greet, 0)
+    lax.fori_loop(1, n, greet, 0, unroll=True)
 
     row = lax.broadcasted_iota(jnp.int32, (planes, LANES), 0)
     lane = lax.broadcasted_iota(jnp.int32, (planes, LANES), 1)
@@ -136,7 +137,7 @@
 
     for load in loads[:3]:
         load.wait()
-    lax.fori_loop(0, chunks, first, 0)
+    lax.fori_loop(0, chunks, first, 0, unroll=UNROLL)
     pl.semaphore_wait(barrier, n - 1)
 
     def state_copy(k, side):
@@ -228,17 +229,12 @@
             outer[side, f] = values[f]
 
     def two_sweeps(s, carry):
-        lax.fori_loop(0, chunks, before, 0)
+        lax.fori_loop(0, chunks, before, 0, unroll=UNROLL)
         for there, come, gone in ((has_low, 0, 1), (has_high, 1, 0)):
             @pl.when(there)
             def _():
                 state_copy(s, come).wait_recv()
                 state_copy(s, gone).wait_send()
-
-            @pl.when(there & (s == 0))
-            def _():
-                fixed_copy(come).wait_recv()
-                fixed_copy(gone).wait_send()
 
         def with_halo(c, inner):
             behind(
@@ -249,10 +245,16 @@
             )
             return inner
 
-        lax.fori_loop(0, chunks, with_halo, 0)
+        lax.fori_loop(0, chunks, with_halo, 0, unroll=UNROLL)
+        lax.fori_loop(0, chunks, before, 0, unroll=UNROLL)
+        for there, come, gone in ((has_low, 0, 1), (has_high, 1, 0)):
+            @pl.when(there & (s == 0))
+            def _():
+                fixed_copy(come).wait_recv()
+                fixed_copy(gone).wait_send()
+
         for side in range(2):
             sweep_outer(s, side)
-        lax.fori_loop(0, chunks, before, 0)
 
         def with_outer(c, inner):
             behind(
@@ -263,7 +265,7 @@
             )
             return inner
 
-        lax.fori_loop(0, chunks, with_outer, 0)
+        lax.fori_loop(0, chunks, with_outer, 0, unroll=UNROLL)
         pl.when(s + 1 < ITERS // 2)(lambda: exchange(s + 1))
         return carry
 
@@ -302,7 +304,7 @@
             pressure[r, c] = total
         return carry
 
-    lax.fori_loop(0, chunks, finish, 0)
+    lax.fori_loop(0, chunks, finish, 0, unroll=UNROLL)
 
     spread = dot_exact(pressure[...].reshape(2 * grid, LANES), pick[...], ((1,), (0,)))
     surface = [
@@ -338,8 +340,8 @@
             copy(d).wait()
             return carry
 
-        lax.fori_loop(1, n, start, 0)
-        lax.fori_loop(1, n, wait, 0)
+        lax.fori_loop(1, n, start, 0, unroll=True)
+        lax.fori_loop(1, n, wait, 0, unroll=True)
 
     landed[0] = tiles[me]
     run(tile_copy)
@@ -370,6 +372,19 @@
     )
 
 
+def hand_over(state, forces, state_out, forces_out, state_held, forces_held, done):
+    routes = ((state, state_held, state_out), (forces, forces_held, forces_out))
+    inward = [pltpu.make_async_copy(a, b, done.at[i]) for i, (a, b, c) in enumerate(routes)]
+    outward = [pltpu.make_async_copy(b, c, done.at[2 + i]) for i, (a, b, c) in enumerate(routes)]
+    for copy in inward:
+        copy.start()
+    for first, second in zip(inward, outward):
+        first.wait()
+        second.start()
+    for copy in outward:
+        copy.wait()
+
+
 def local(
     rhs, inv_diag, face_coef, flux_jac, press_weights, surface_cells, interface_slot, mode_shapes
 ):
@@ -384,7 +399,7 @@
     smem = pl.BlockSpec(memory_space=pltpu.SMEM)
     f32 = jnp.float32
     dma = pltpu.SemaphoreType.DMA
-    return pl.pallas_call(
+    state, forces = pl.pallas_call(
         functools.partial(kernel, n),
         out_shape=(
             jax.ShapeDtypeStruct(rhs.shape, f32),
@@ -426,6 +441,17 @@
         flux_jac.transpose(1, 0, 2), press_weights, rhs, inv_diag, face_coef,
         surface_cells.reshape(1, rows), interface_slot.reshape(1, rows), mode_shapes.T,
     )
+    return pl.pallas_call(
+        hand_over,
+        out_shape=(
+            jax.ShapeDtypeStruct(state.shape, f32),
+            jax.ShapeDtypeStruct(forces.shape, f32),
+        ),
+        in_specs=[hbm, hbm],
+        out_specs=(hbm, hbm),
+        scratch_shapes=[pltpu.VMEM(state.shape, f32), pltpu.VMEM(forces.shape, f32), dma((4,))],
+        compiler_params=pltpu.CompilerParams(vmem_limit_bytes=63 * 2**20),
+    )(state, forces)
 
 
 def solution(mesh):

time: 48 us -> 44.1 us (0.919)
  local copies, waits for them, and re-layouts: 2.96 us -> 0 us
  Pallas kernels: 44.2 us -> 43.3 us
    unnamed x2 -> x0, local copies, waits for them, and re-layouts: 2.96 us -> none
    pallas_call x1, Pallas kernels: 44.2 us -> 41.5 us  [local(): pl.pallas_call(functools.partial(kernel, n), out_shape=(jax.ShapeDtypeStr...]
    pallas_call x0 -> x1, Pallas kernels: none -> 1.73 us  [local(): pl.pallas_call(hand_over, out_shape=(jax.ShapeDtypeStruct(state.shape, f3...]
where the time goes in v3:
time: 44.1 us; the launch traced here: 43.9 us
  Pallas kernels  43.3 us (98%)
  between operations  0.64 us (1%)
    pallas_call x1, Pallas kernels, local(): pl.pallas_call(functools.partial(kernel, n), out_shape=(jax.ShapeDtypeStr...  41.5 us
    pallas_call x1, Pallas kernels, local(): pl.pallas_call(hand_over, out_shape=(jax.ShapeDtypeStruct(state.shape, f3...  1.73 us

profile of v3, /device:TPU:0, one launch (start us, length us, event | category | flops | bytes accessed | tf_op | source)
XLA Modules:
  0.0 43.9 jit_solution(8044423789894379857)
XLA Ops:
  0.6 41.5 %shard_map.95 = (f32[2,5,8,1024]{3,2,1,0:T(8,128)}, f32[2,12]{1,0:T(2,128)}) custom-call(f32[5,2,5]{2,1,0:T(2,128)} %bitcast.5, f32[5]{0:T(128)} %press.1, f32[2,5,8,1024]{3,2,1,0:T(8,128)} %rhs_in.1, f32[2,5,5,8,1024]{4,3,2,1,0:T(8,128)} %inv_in.1, f32[4,8,1024]{2,1,0:T(8,128)} %face_in.1, s32[1,512]{1,0:T(1,128)} %bitcast.6, s32[1,512]{1,0:T(1,128)} %bitcast.7, ...), custom_call_target="tpu_custom_call" | custom-call | tf_op jit(solution)/shard_map/pallas_call | solution.py:402
  42.2 1.7 %shard_map.96 = (f32[2,5,8,1024]{3,2,1,0:T(8,128)}, f32[2,12]{1,0:T(2,128)}) custom-call(f32[2,5,8,1024]{3,2,1,0:T(8,128)} %get-tuple-element.4.state, f32[2,12]{1,0:T(2,128)} %get-tuple-element.5.forces), custom_call_target="tpu_custom_call" | custom-call | tf_op jit(solution)/shard_map/pallas_call | solution.py:444

commit v4 on v3

--- a/solution.py
+++ b/solution.py
@@ -140,10 +140,10 @@
     lax.fori_loop(0, chunks, first, 0, unroll=UNROLL)
     pl.semaphore_wait(barrier, n - 1)
 
-    def state_copy(k, side):
+    def state_copy(k, side, p):
         return pltpu.make_async_remote_copy(
-            src_ref=send.at[k, side], dst_ref=halo.at[k, side],
-            send_sem=halo_send.at[k, side], recv_sem=halo_recv.at[k, side],
+            src_ref=send.at[k, side, p], dst_ref=halo.at[k, side, p],
+            send_sem=halo_send.at[k, side, p], recv_sem=halo_recv.at[k, side, p],
             device_id={"space": me + 1 - 2 * side}, device_id_type=MESH,
         )
 
@@ -155,8 +155,9 @@
         )
 
     def exchange(k):
-        for side, there in ((0, has_high), (1, has_low)):
-            pl.when(there)(state_copy(k, side).start)
+        for p in range(2):
+            for side, there in ((0, has_high), (1, has_low)):
+                pl.when(there)(state_copy(k, side, p).start)
 
     exchange(0)
     for side, there in ((0, has_high), (1, has_low)):
@@ -233,8 +234,7 @@
         for there, come, gone in ((has_low, 0, 1), (has_high, 1, 0)):
             @pl.when(there)
             def _():
-                state_copy(s, come).wait_recv()
-                state_copy(s, gone).wait_send()
+                state_copy(s, come, 0).wait_recv()
 
         def with_halo(c, inner):
             behind(
@@ -248,6 +248,12 @@
         lax.fori_loop(0, chunks, with_halo, 0, unroll=UNROLL)
         lax.fori_loop(0, chunks, before, 0, unroll=UNROLL)
         for there, come, gone in ((has_low, 0, 1), (has_high, 1, 0)):
+            @pl.when(there)
+            def _():
+                state_copy(s, come, 1).wait_recv()
+                state_copy(s, gone, 0).wait_send()
+                state_copy(s, gone, 1).wait_send()
+
             @pl.when(there & (s == 0))
             def _():
                 fixed_copy(come).wait_recv()
@@ -432,7 +438,7 @@
             pltpu.VMEM((n, tall, LANES), f32),
             pltpu.VMEM((2, padded), f32),
             pltpu.VMEM((n, 2, padded), f32),
-            dma((ITERS // 2, 2)), dma((ITERS // 2, 2)), dma((2,)), dma((2,)), dma((n,)), dma((n,)), dma((n,)), dma((n,)),
+            dma((ITERS // 2, 2, 2)), dma((ITERS // 2, 2, 2)), dma((2,)), dma((2,)), dma((n,)), dma((n,)), dma((n,)), dma((n,)),
         ],
         compiler_params=pltpu.CompilerParams(
             collective_id=0, has_side_effects=True, vmem_limit_bytes=63 * 2**20

time: 44.1 us -> 42.7 us (0.968)
  Pallas kernels: 43.3 us -> 41.8 us
    pallas_call x1, Pallas kernels: 41.5 us -> 40.1 us  [local(): pl.pallas_call(functools.partial(kernel, n), out_shape=(jax.ShapeDtypeStr...]
where the time goes in v4:
time: 42.7 us; the launch traced here: 42.5 us
  Pallas kernels  41.8 us (98%)
  between operations  0.64 us (1%)
    pallas_call x1, Pallas kernels, local(): pl.pallas_call(functools.partial(kernel, n), out_shape=(jax.ShapeDtypeStr...  40.1 us
    pallas_call x1, Pallas kernels, local(): pl.pallas_call(hand_over, out_shape=(jax.ShapeDtypeStruct(state.shape, f3...  1.73 us

profile of v4, /device:TPU:0, one launch (start us, length us, event | category | flops | bytes accessed | tf_op | source)
XLA Modules:
  0.0 42.5 jit_solution(7445126533131680127)
XLA Ops:
  0.6 40.1 %shard_map.95 = (f32[2,5,8,1024]{3,2,1,0:T(8,128)}, f32[2,12]{1,0:T(2,128)}) custom-call(f32[5,2,5]{2,1,0:T(2,128)} %bitcast.5, f32[5]{0:T(128)} %press.1, f32[2,5,8,1024]{3,2,1,0:T(8,128)} %rhs_in.1, f32[2,5,5,8,1024]{4,3,2,1,0:T(8,128)} %inv_in.1, f32[4,8,1024]{2,1,0:T(8,128)} %face_in.1, s32[1,512]{1,0:T(1,128)} %bitcast.6, s32[1,512]{1,0:T(1,128)} %bitcast.7, ...), custom_call_target="tpu_custom_call" | custom-call | tf_op jit(solution)/shard_map/pallas_call | solution.py:408
  40.7 1.7 %shard_map.96 = (f32[2,5,8,1024]{3,2,1,0:T(8,128)}, f32[2,12]{1,0:T(2,128)}) custom-call(f32[2,5,8,1024]{3,2,1,0:T(8,128)} %get-tuple-element.4.state, f32[2,12]{1,0:T(2,128)} %get-tuple-element.5.forces), custom_call_target="tpu_custom_call" | custom-call | tf_op jit(solution)/shard_map/pallas_call | solution.py:450
